TPU v7x, 512 devices: a whole 4x8x8 slice. The times are simulated.
512 devices in a mesh: rep: 16 (over y, z_lo), head: 32 (over z_hi, x, core).
Axes of the slice: x: 4, y: 8, z: 8 (z_hi: 4, z_lo: 2; z = z_hi * 2 + z_lo), core: 2. Of those that a mesh axis runs over, the one named last changes fastest.
Arguments:
- step_hidden: bfloat16 [80, 12288], P(None, 'rep')
- paused_hidden: bfloat16 [1792, 12288], P('head', 'rep')
- ln_gain: float32 [12288], P('rep'), may hold values from 0.1 to 1.9
- ln_bias: float32 [12288], P('rep'), may hold values from -3 to 3
- w_query: bfloat16 [12288, 8192], P('rep', 'head')
- w_keyval: bfloat16 [12288, 2, 8192], P('rep', None, 'head'), may hold values from -0.0546875 to 0.0546875
- w_out: bfloat16 [8192, 12288], P('head', 'rep'), may hold values from -0.5 to 0.5
- cache: bfloat16 [64, 2, 512, 8192], P('rep', None, None, 'head'), may hold values from -6 to 6
- cache_lengths: int32 [64], P('rep'), may hold values from 1 to 512, as said below
- partner: int32 [16], replicated, may hold values from 0 to 15, each once
- paused_count: int32 [16], replicated, may hold values from 1 to 112, as said below
Outputs:
- paused_keyval: bfloat16 [1792, 2, 8192], P('rep', None, 'head')
- attention_update: bfloat16 [80, 12288], P(None, 'rep')
Inputs may be any that keep to these rules, and one draw needn't show every extreme that they name: `cache_lengths`: every resident sequence has at least one valid slot; some sequence fills all 512. `partner`: A permutation of the sequence groups. `paused_count`: some group's paused sequence fills all 112 slots.
All inputs are finite; a program needn't handle non-finite values.
Results may differ from a plain program's by a relative error of at most 0.012.
The roundings to bfloat16 on the way count: a program that leaves them out, or rounds other values in their place, can miss the bound.
Values may be sent and summed in bfloat16 or wider, within the bound.
A program may use at most 64 MiB of HBM per device.

v0:
```python
import math

import jax
import jax.numpy as jnp
from jax import lax
from jax.sharding import PartitionSpec as P

D = 12288
HEAD_DIM = 128
MIG = 112


def moments(values):
    wide = values.astype(jnp.float32)
    return (jnp.sum(wide, axis=1), jnp.sum(wide * wide, axis=1))


def normalize(values, total, square, ln_gain, ln_bias):
    center = total / D
    spread = square / D - center * center
    scale = lax.rsqrt(spread + 1e-05)
    wide = values.astype(jnp.float32)
    return ((wide - center[:, None]) * scale[:, None] * ln_gain + ln_bias).astype(jnp.bfloat16)


def attend(query, keys, values, lengths, own_key, own_value):
    factor = 1.0 / math.sqrt(HEAD_DIM)
    scores = jnp.einsum("nhd,nchd->nhc", query, keys, preferred_element_type=jnp.float32) * factor
    own = jnp.sum(query.astype(jnp.float32) * own_key.astype(jnp.float32), axis=2) * factor
    valid = jnp.arange(keys.shape[1], dtype=jnp.int32)[None, :] < lengths[:, None]
    scores = jnp.where(valid[:, None, :], scores, -jnp.inf)
    top = jnp.maximum(jnp.max(scores, axis=2), own)
    expo_cache = jnp.exp(scores - top[:, :, None])
    expo_own = jnp.exp(own - top)
    total = jnp.sum(expo_cache, axis=2) + expo_own
    weight_cache = (expo_cache / total[:, :, None]).astype(jnp.bfloat16)
    weight_own = (expo_own / total).astype(jnp.bfloat16)
    mixed = jnp.einsum("nhc,nchd->nhd", weight_cache, values, preferred_element_type=jnp.float32)
    return mixed + weight_own.astype(jnp.float32)[:, :, None] * own_value.astype(jnp.float32)


def on_device(
    step_hidden,
    paused_hidden,
    ln_gain,
    ln_bias,
    w_query,
    w_keyval,
    w_out,
    cache,
    cache_lengths,
    partner,
    paused_count,
):
    paused_total, paused_square = moments(paused_hidden)
    step_total, step_square = moments(step_hidden)
    paused_total, paused_square, step_total, step_square = lax.psum(
        (paused_total, paused_square, step_total, step_square), "rep"
    )
    normed_paused = normalize(paused_hidden, paused_total, paused_square, ln_gain, ln_bias)
    normed_step = normalize(step_hidden, step_total, step_square, ln_gain, ln_bias)
    rep_index = lax.axis_index("rep")
    live_count = paused_count[partner[rep_index]]
    local_width = w_query.shape[1]
    local_heads = local_width // HEAD_DIM
    resident_count = cache.shape[0]
    slots = cache.shape[2]
    query_part = jnp.dot(normed_step, w_query, preferred_element_type=jnp.float32)
    keyval_part = jnp.einsum(
        "nd,dkw->nkw", normed_step, w_keyval, preferred_element_type=jnp.float32
    )
    query_rows, keyval_rows = (
        lax.psum_scatter(query_part, "rep", scatter_dimension=0, tiled=True),
        lax.psum_scatter(keyval_part, "rep", scatter_dimension=0, tiled=True),
    )
    query_rows = query_rows.astype(jnp.bfloat16).reshape(-1, local_heads, HEAD_DIM)
    keyval_rows = keyval_rows.astype(jnp.bfloat16).reshape(-1, 2, local_heads, HEAD_DIM)
    gathered = lax.all_gather(normed_paused, "head", axis=0, tiled=True)
    per_device = gathered.shape[0] // lax.axis_size("rep")
    place = jnp.arange(lax.axis_size("rep") * per_device, dtype=jnp.int32)
    source = jnp.take(partner, place // MIG) * MIG + place % MIG
    picked = jnp.take(gathered, source, axis=0)
    sums = lax.psum_scatter(
        jnp.einsum("nd,dkw->nkw", picked, w_keyval, preferred_element_type=jnp.float32),
        "rep",
        scatter_dimension=0,
        tiled=True,
    )
    live = jnp.arange(per_device, dtype=jnp.int32)[:, None, None] < live_count
    paused_keyval = jnp.where(live, sums, 0.0).astype(jnp.bfloat16)
    keys = cache[:, 0].reshape(resident_count, slots, local_heads, HEAD_DIM)
    values = cache[:, 1].reshape(resident_count, slots, local_heads, HEAD_DIM)
    resident = attend(
        query_rows[:resident_count],
        keys,
        values,
        cache_lengths,
        keyval_rows[:resident_count, 0],
        keyval_rows[:resident_count, 1],
    )
    paused_count_local = paused_keyval.shape[0]
    migrated_keys = paused_keyval[:, 0].reshape(1, paused_count_local, local_heads, HEAD_DIM)
    migrated_values = paused_keyval[:, 1].reshape(1, paused_count_local, local_heads, HEAD_DIM)
    migrated = attend(
        query_rows[resident_count:],
        migrated_keys,
        migrated_values,
        live_count[None],
        keyval_rows[resident_count:, 0],
        keyval_rows[resident_count:, 1],
    )
    mixed = (
        jnp.concatenate([resident, migrated], axis=0).reshape(-1, local_width).astype(jnp.bfloat16)
    )
    partial_update = jnp.dot(
        lax.all_gather(mixed, "rep", axis=0, tiled=True), w_out, preferred_element_type=jnp.float32
    )
    attention_update = lax.psum(partial_update, "head").astype(jnp.bfloat16)
    return (paused_keyval, attention_update)


def solution(mesh):
    in_specs = (
        P(None, "rep"),
        P("head", "rep"),
        P("rep"),
        P("rep"),
        P("rep", "head"),
        P("rep", None, "head"),
        P("head", "rep"),
        P("rep", None, None, "head"),
        P("rep"),
        P(),
        P(),
    )
    out_specs = (P("rep", None, "head"), P(None, "rep"))
    return jax.shard_map(
        on_device, mesh=mesh, in_specs=in_specs, out_specs=out_specs, check_vma=False
    )
```

profile of v0, /device:TPU:1, one launch (start us, length us, event | category | flops | bytes accessed | tf_op | source)
XLA Modules:
  0.0 456.5 jit_solution(5082137808343422650)
XLA Ops:
  7.2 1.1 convert_reduce_fusion
  8.3 29.8 %all-reduce.3 = (f32[80]{0:T(128)S(1)}, f32[80]{0:T(128)S(1)}) all-reduce(f32[80]{0:T(128)S(1)} %get-tuple-element.13, f32[80]{0:T(128)S(1)} %get-tuple-element.12), channel_id=1, replica_groups=mesh['rep'=16,'head'=32] {'rep'}, use_global_device_ids=true, to_apply=%region_8.0 | all-reduce | flops 160 | bytes 1280 | tf_op jit(solution)/shard_map/psum | solution.py:57
  38.2 1.2 fusion.7
  39.6 1.3 fusion.60
  40.9 1.0 convert_reduce_fusion.1
  41.9 49.5 %all-reduce.6 = (f32[56]{0:T(128)S(1)}, f32[56]{0:T(128)S(1)}, bf16[80,256]{1,0:T(8,128)(2,1)}, bf16[80,2,256]{2,1,0:T(2,128)(2,1)}) all-reduce(f32[56]{0:T(128)S(1)} %get-tuple-element.15, f32[56]{0:T(128)S(1)} %get-tuple-element.14, f32[80,256]{1,0:T(8,128)S(1)} %fusion.60, ...), channel_id=1, replica_groups=mesh['rep'=16,'head'=32] {'rep'}, use_global_device_ids=true, to_apply=%region_3.0 | all-reduce | flops 61552 | bytes 369536 | tf_op jit(solution)/shard_map/psum | solution.py:57
  91.4 1.4 fusion.18
  94.3 4.4 fusion.38
  98.7 5.4 %compare_and_fusion = (pred[1792]{0:T(1024)(128)(4,1)S(1)}, s32[1792]{0:T(1024)S(1)}) fusion(pred[1792]{0:T(1024)(128)(4,1)S(1)} %compare_reduce_fusion, pred[1792]{0:T(1024)(128)(4,1)S(1)} %compare_reduce_fusion.1, pred[1792]{0:T(1024)(128)(4,1)S(1)} %compare_reduce_fusion.2, pred[1792]{0:T(1024)(128)(4,1)S(1)} %compare_reduce_fusion.3, ...), kind=kLoop, calls=%fused_computation.82 | loop fusion | flops 64512 | bytes 32292 | tf_op jit(solution)/shard_map/jit(_take)/and | solution.py:82
  104.2 73.5 %all-gather.3.cloned.1.call-done = bf16[1792,768]{1,0:T(8,128)(2,1)} async-done(((bf16[56,768]{1,0:T(8,128)(2,1)}), bf16[1792,768]{1,0:T(8,128)(2,1)}) %all-gather.3.cloned.1.call-update) | async-done | bytes 2752528 | tf_op jit(solution)/shard_map/all_gather | solution.py:78
  177.7 9.1 %gather_fusion = bf16[1792,768]{1,0:T(8,128)(2,1)S(1)} fusion(bf16[1792,768]{1,0:T(8,128)(2,1)} %all-gather.3.cloned.1.call-done, s32[2048]{0:T(1024)S(1)} %pad_clamp_fusion), kind=kCustom, calls=%fused_computation | custom fusion | bytes 5512192 | tf_op jit(solution)/shard_map/jit(_take)/gather | solution.py:82
  186.8 3.5 fusion
  190.4 1.3 dynamic-slice
  192.3 0.7 dynamic-slice_convert_fusion.1
  194.3 0.7 dynamic-slice_convert_fusion
  195.2 2.6 fusion.62
  197.9 1.5 copy.48
  199.4 1.1 reshape_squeeze.9
  201.3 1.5 fusion.5
  205.0 72.7 %reduce-scatter.2.cloned.1.call-done = f32[112,2,256]{2,0,1:T(8,128)} async-done(((f32[1792,2,256]{2,0,1:T(8,128)}), f32[112,2,256]{2,0,1:T(8,128)}) %reduce-scatter.2.cloned.1.call-update) | async-done | bytes 229392 | tf_op jit(solution)/shard_map/reduce_scatter | solution.py:83
  277.6 1.0 select_convert_fusion
  278.7 0.7 copy.35
  280.3 24.8 %all-gather = bf16[16,5,256]{2,1,0:T(8,128)(2,1)S(1)} all-gather(bf16[1,5,256]{2,1,0:T(8,128)(2,1)S(1)} %maximum_bitcast_fusion), channel_id=1, replica_groups=mesh['rep'=16,'head'=32] {'rep'}, dimensions={0}, use_global_device_ids=true | all-gather | bytes 43520 | tf_op jit(solution)/shard_map/all_gather | solution.py:116
  305.3 144.3 %all-reduce.7 = bf16[80,768]{1,0:T(8,128)(2,1)} all-reduce(f32[80,768]{1,0:T(8,128)S(1)} %fusion.66), channel_id=1, replica_groups=mesh['rep'=16,'head'=32] {'head'}, use_global_device_ids=true, to_apply=%region_17.18 | all-reduce | flops 61440 | bytes 368640 | tf_op jit(solution)/shard_map/psum | solution.py:118
  (66 shorter events, 5.2 us)
Async XLA Ops:
  7.2 31.0 %copy-start = (bf16[768,2,256]{2,1,0:T(2,128)(2,1)S(1)}, bf16[768,2,256]{2,1,0:T(2,128)(2,1)}, u32[]{:S(2)}) copy-start(bf16[768,2,256]{2,1,0:T(2,128)(2,1)} %param.16) | copy-start | bytes 2359300
  7.2 84.3 %copy-start.2 = (bf16[56,768]{1,0:T(8,128)(2,1)S(1)}, bf16[56,768]{1,0:T(8,128)(2,1)}, u32[]{:S(2)}) copy-start(bf16[56,768]{1,0:T(8,128)(2,1)} %param.12) | copy-start | bytes 258052
  7.2 86.4 %copy-start.3 = (s32[16]{0:T(128)S(1)}, s32[16]{0:T(128)}, u32[]{:S(2)}) copy-start(s32[16]{0:T(128)} %param.20) | copy-start | bytes 196
  7.2 170.5 %all-gather.3.cloned.1.call-start = ((), (), s32[]{:S(2)}) async-start(), calls=%async_computation.1 | async-start | bytes 2838528 | tf_op jit(solution)/shard_map/all_gather | solution.py:78
  92.9 184.7 %reduce-scatter.2.cloned.1.call-start = ((), (), s32[]{:S(2)}) async-start(), calls=%async_computation.2 | async-start | bytes 3899392 | tf_op jit(solution)/shard_map/reduce_scatter | solution.py:83
  197.9 2.6 copy-start.4
  197.9 5.7 %copy-start.5 = (s32[16]{0:T(128)S(1)}, s32[16]{0:T(128)}, u32[]{:S(2)}) copy-start(s32[16]{0:T(128)} %param.21) | copy-start | bytes 196
  199.4 105.7 %copy-start.1 = (bf16[256,768]{1,0:T(8,128)(2,1)S(1)}, bf16[256,768]{1,0:T(8,128)(2,1)}, u32[]{:S(2)}) copy-start(bf16[256,768]{1,0:T(8,128)(2,1)} %param.17) | copy-start | bytes 1179652
Sparse Core Ops, SparseCore 0:
  93.0 84.6 all-gather.2
  190.5 87.0 reduce-scatter.1
where the time goes:
time: 461 us; the launch traced here: 456 us
  blocking collectives  248 us (54%)
  waiting for transfers between devices  146 us (32%)
  local copies, waits for them, and re-layouts  19.6 us (4%)
  other arithmetic  17 us (4%)
  between operations  16.8 us (4%)
  matrix products  8.32 us (2%)
    psum x1, blocking collectives, on_device(): attention_update = lax.psum(partial_update, 'head').astype(jnp.bfloat16)  144 us
    psum x2, blocking collectives, on_device(): lax.psum((paused_total, paused_square, step_total, step_square), 'rep')  79.3 us
    all_gather x1, waiting for transfers between devices, on_device(): gathered = lax.all_gather(normed_paused, 'head', axis=0, tiled=True)  73.5 us
    reduce_scatter x1, waiting for transfers between devices, on_device(): lax.psum_scatter(jnp.einsum('nd,dkw->nkw', picked, w_keyval, preferred_el...  72.7 us
    all_gather x1, blocking collectives, on_device(): lax.all_gather(mixed, 'rep', axis=0, tiled=True)  24.8 us
  transfers between devices with their start and end apart: 2, of which 2 were waited for; matrix products, arithmetic and copies ran while one was open for 5% of the time, Pallas kernels for 0%

commit v1 on v0

v1 whole, which is shorter than its diff:
```python
import math

import jax
import jax.numpy as jnp
from jax import lax
from jax.experimental import pallas as pl
from jax.experimental.pallas import tpu as pltpu
from jax.sharding import PartitionSpec as P

D = 12288
HEAD_DIM = 128
MIG = 112
MESH = pl.DeviceIdType.MESH
F32 = jnp.float32
BF16 = jnp.bfloat16

REP = 16
HEAD = 32
FEATS = D // REP
HALF = MIG // 2
ROWS = 80
NQ = 5
FACTOR = 1.0 / math.sqrt(HEAD_DIM)


def rows_of(shape):
    return lax.broadcasted_iota(jnp.int32, shape, len(shape) - 2)


def lanes_of(shape):
    return lax.broadcasted_iota(jnp.int32, shape, len(shape) - 1)


def wait_bytes(ref, sem):
    pltpu.make_async_copy(ref, ref, sem).wait()


def kernel(
    partner,
    paused_count,
    lengths,
    step_ref,
    paused_ref,
    gain_ref,
    bias_ref,
    w_query_hbm,
    w_keyval_hbm,
    w_out_hbm,
    cache_hbm,
    keyval_out,
    update_out,
    w_all,
    w_out,
    cache,
    stats,
    gathered,
    partial,
    step_send,
    step_recv,
    ring_send,
    ring_recv,
    pair_send,
    pair_recv,
    mixed_all,
    upd_send,
    upd_recv,
    final,
    load_sem,
    stats_sems,
    ag_send,
    ag_recv,
    step_sems,
    ring_ssem,
    ring_rsem,
    pair_ssem,
    pair_rsem,
    mixed_sems,
    upd_sems,
    final_sems,
):
    rep = lax.axis_index("rep")
    head = lax.axis_index("head")
    y, zl = rep // 2, lax.rem(rep, 2)
    core = lax.rem(head, 2)
    chip = head // 2
    zh, x = chip // 4, lax.rem(chip, 4)

    barrier = pltpu.get_barrier_semaphore()

    def greet_rep(d, carry):
        pl.semaphore_signal(
            barrier, inc=1, device_id=(lax.rem(rep + d, REP), head), device_id_type=MESH
        )
        return carry

    def greet_head(d, carry):
        pl.semaphore_signal(
            barrier, inc=1, device_id=(rep, lax.rem(head + d, HEAD)), device_id_type=MESH
        )
        return carry

    lax.fori_loop(1, REP, greet_rep, 0)
    lax.fori_loop(1, HEAD, greet_head, 0)

    loads = [
        pltpu.make_async_copy(w_query_hbm, w_all.at[:, pl.ds(0, 256)], load_sem.at[0]),
        pltpu.make_async_copy(w_keyval_hbm, w_all.at[:, pl.ds(256, 512)], load_sem.at[1]),
        pltpu.make_async_copy(cache_hbm, cache, load_sem.at[2]),
        pltpu.make_async_copy(w_out_hbm, w_out, load_sem.at[3]),
    ]
    for load in loads:
        load.start()

    def all_peers(axis_size, me, sends):
        def body(d, carry):
            sends(lax.rem(me + d, axis_size))
            return carry

        lax.fori_loop(1, axis_size, body, 0)

    def local_stats(values):
        wide = values.astype(F32)
        mean = jnp.sum(wide, axis=1, keepdims=True) / FEATS
        offset = wide - mean
        return mean, jnp.sum(offset * offset, axis=1, keepdims=True)

    def place(pair, lane, rows):
        lanes = lanes_of((rows, 128))
        block = jnp.where(lanes == lane, pair[0], jnp.where(lanes == lane + 1, pair[1], 0.0))
        return jnp.concatenate([block, jnp.zeros((128 - rows, 128), F32)], axis=0)

    packed = place(local_stats(step_ref[...]), 0, ROWS) + place(
        local_stats(paused_ref[...]), 2, HALF
    )
    stats[rep] = jnp.transpose(packed)[:8]

    pl.semaphore_wait(barrier, REP + HEAD - 2)

    def send_stats(peer):
        pltpu.make_async_remote_copy(
            src_ref=stats.at[rep],
            dst_ref=stats.at[rep],
            send_sem=stats_sems.at[0],
            recv_sem=stats_sems.at[1],
            device_id=(peer, head),
            device_id_type=MESH,
        ).start()

    all_peers(REP, rep, send_stats)
    wait_bytes(stats.at[pl.ds(0, REP - 1)], stats_sems.at[1])

    every = stats[...]
    mean = jnp.sum(every, axis=0) / REP
    away = every - mean[None]
    away = jnp.sum(away * away, axis=0)
    sums = mean * REP

    def scale_of(row):
        spread = (sums[row + 1 : row + 2] + FEATS * away[row : row + 1]) / D
        return lax.rsqrt(spread + 1e-05)

    columns = jnp.transpose(
        jnp.concatenate(
            [mean[0:1], scale_of(0), mean[2:3], scale_of(2), jnp.zeros((4, 128), F32)], axis=0
        )
    )

    def normalize(values, lane, rows):
        center = columns[:rows, lane : lane + 1]
        scale = columns[:rows, lane + 1 : lane + 2]
        return ((values.astype(F32) - center) * scale * gain_ref[...] + bias_ref[...]).astype(BF16)

    normed_paused = normalize(paused_ref[...], 2, HALF).astype(F32)
    gathered[head] = jnp.concatenate(
        [normed_paused, jnp.zeros((8, FEATS), F32)], axis=0
    ).astype(BF16)

    def slot(jz, jx, c):
        return (lax.rem(zh + jz + 4, 4) * 4 + lax.rem(x + jx + 4, 4)) * 2 + c

    sent = []

    def pass_on(jz, jx, tz, tx, to_core):
        where = slot(jz, jx, core)
        target = slot(tz, tx, 1 - core if to_core else core)
        copy = pltpu.make_async_remote_copy(
            src_ref=gathered.at[where],
            dst_ref=gathered.at[where],
            send_sem=ag_send.at[len(sent)],
            recv_sem=ag_recv.at[where],
            device_id=(rep, target),
            device_id_type=MESH,
        )
        copy.start()
        sent.append(copy)

    def arrive(where):
        wait_bytes(gathered.at[where], ag_recv.at[where])

    pass_on(0, 0, 1, 0, False)
    pass_on(0, 0, -1, 0, False)
    pass_on(0, 0, 0, 1, False)
    pass_on(0, 0, 0, -1, False)
    pass_on(0, 0, 0, 0, True)

    normed_step = normalize(step_ref[...], 0, ROWS)
    row, col = rows_of((128, ROWS)), lanes_of((128, ROWS))
    spread_rows = jnp.where((row // 8) * NQ + lax.rem(row, 8) == col, 1.0, 0.0)
    spread_rows = jnp.where(lax.rem(row, 8) < NQ, spread_rows, 0.0).astype(BF16)
    padded_step = jnp.dot(spread_rows, normed_step, preferred_element_type=F32).astype(BF16)
    loads[0].wait()
    loads[1].wait()
    step_part = jnp.dot(padded_step, w_all[...], preferred_element_type=F32)
    step_send[...] = step_part.reshape(REP, 8, FEATS)
    step_recv[rep] = step_send[rep]

    def send_step(peer):
        pltpu.make_async_remote_copy(
            src_ref=step_send.at[peer],
            dst_ref=step_recv.at[rep],
            send_sem=step_sems.at[0],
            recv_sem=step_sems.at[1],
            device_id=(peer, head),
            device_id_type=MESH,
        ).start()

    all_peers(REP, rep, send_step)

    for jz, jx in (
        (-1, 0),
        (1, 0),
        (0, -1),
        (0, 1),
        (2, 0),
        (-1, -1),
        (-1, 1),
        (1, -1),
        (1, 1),
        (0, 2),
        (2, -1),
        (2, 1),
        (-1, 2),
        (1, 2),
        (2, 2),
    ):
        arrive(slot(jz, jx, core))
        if jx == 0:
            if jz == -1:
                pass_on(jz, jx, 1, 0, False)
            pass_on(jz, jx, 0, 1, False)
            pass_on(jz, jx, 0, -1, False)
        if jx == -1 and jz in (0, 2):
            pass_on(jz, jx, 0, 1, False)
        if jx == 1 and jz in (-1, 1):
            pass_on(jz, jx, 0, -1, False)
        pass_on(jz, jx, 0, 0, True)

    def arrive_other(i, carry):
        arrive(i * 2 + 1 - core)
        return carry

    lax.fori_loop(0, 16, arrive_other, 0)

    def project(i, carry):
        rows = gathered[pl.ds(i * 8, 8)].reshape(512, FEATS)
        part = jnp.dot(rows, w_all[:, 256:], preferred_element_type=F32).reshape(4, 2, 64, 512)
        for j in range(4):
            partial[i * 4 + j, 0:HALF] = part[j, 0, 0:HALF]
            partial[i * 4 + j, HALF:MIG] = part[j, 1, 0:HALF]
        return carry

    lax.fori_loop(0, 4, project, 0)

    def own_part(to_y, k):
        blocks = []
        for z in range(2):
            group = partner[to_y * 2 + z]
            blocks.append(partial[group, :, k * 256 : (k + 1) * 256])
        return jnp.concatenate(blocks, axis=0)

    def ring_step(way, k, s):
        steps = 4 if way == k else 3
        sign = 1 if way == 0 else -1
        block = own_part(lax.rem(y + sign * (steps - s) + 8, 8), k)
        if s > 0:
            wait_bytes(ring_recv.at[way, k, s - 1], ring_rsem.at[way, k, s - 1])
            block = block + ring_recv[way, k, s - 1].astype(F32)
        ring_send[way, k, s] = block.astype(BF16)
        copy = pltpu.make_async_remote_copy(
            src_ref=ring_send.at[way, k, s],
            dst_ref=ring_recv.at[way, k, s],
            send_sem=ring_ssem.at[way, k, s],
            recv_sem=ring_rsem.at[way, k, s],
            device_id=(lax.rem(y + sign + 8, 8) * 2 + zl, head),
            device_id_type=MESH,
        )
        copy.start()
        sent.append(copy)

    for s in range(4):
        for k in range(2):
            for way in range(2):
                if s < (4 if way == k else 3):
                    ring_step(way, k, s)
        if s == 0:
            wait_bytes(step_recv.at[pl.ds(0, REP - 1)], step_sems.at[1])
            step_qkv = jnp.sum(step_recv[...], axis=0).astype(BF16)
            loads[2].wait()

            def weigh(scores, own, valid):
                scores = jnp.where(valid, scores, -jnp.inf)
                top = jnp.maximum(jnp.max(scores, axis=1, keepdims=True), own)
                expo = jnp.exp(scores - top)
                expo_own = jnp.exp(own - top)
                total = jnp.sum(expo, axis=1, keepdims=True) + expo_own
                return (expo / total).astype(BF16), (expo_own / total).astype(BF16).astype(F32)

            def take(part, h):
                start = part * 256 + h * HEAD_DIM
                return step_qkv[:, start : start + HEAD_DIM]

            def own_score(h):
                return (
                    jnp.sum(take(0, h).astype(F32) * take(1, h).astype(F32), axis=1, keepdims=True)
                    * FACTOR
                )

            def score(query, keys):
                return (
                    lax.dot_general(
                        query, keys, (((1,), (1,)), ((), ())), preferred_element_type=F32
                    )
                    * FACTOR
                )

            resident = []
            row = rows_of((8, 512))
            limit = jnp.zeros((8, 512), jnp.int32)
            for b in range(4):
                limit = jnp.where(row == b, lengths[b], limit)
            valid = lanes_of((8, 512)) < limit
            token = rows_of((8, HEAD_DIM))
            for h in range(2):
                span = slice(h * HEAD_DIM, (h + 1) * HEAD_DIM)
                scores = jnp.zeros((8, 512), F32)
                for b in range(4):
                    scores = jnp.where(row == b, score(take(0, h), cache[b, 0, :, span]), scores)
                weights, weight_own = weigh(scores, own_score(h), valid)
                mixed = jnp.zeros((8, HEAD_DIM), F32)
                for b in range(4):
                    found = jnp.dot(weights, cache[b, 1, :, span], preferred_element_type=F32)
                    mixed = jnp.where(token == b, found, mixed)
                resident.append(mixed + weight_own * take(2, h).astype(F32))

    totals = []
    for k in range(2):
        block = own_part(y, k)
        for way in range(2):
            last = (4 if way == k else 3) - 1
            wait_bytes(ring_recv.at[way, k, last], ring_rsem.at[way, k, last])
            block = block + ring_recv[way, k, last].astype(F32)
        low, high = block[:MIG], block[MIG:]
        totals.append(jnp.where(zl == 0, low, high))
        pair_send[k] = jnp.where(zl == 0, high, low).astype(BF16)
        copy = pltpu.make_async_remote_copy(
            src_ref=pair_send.at[k],
            dst_ref=pair_recv.at[k],
            send_sem=pair_ssem.at[k],
            recv_sem=pair_rsem.at[k],
            device_id=(y * 2 + 1 - zl, head),
            device_id_type=MESH,
        )
        copy.start()
        sent.append(copy)
    live = paused_count[partner[rep]]
    keyval = []
    for k in range(2):
        wait_bytes(pair_recv.at[k], pair_rsem.at[k])
        block = totals[k] + pair_recv[k].astype(F32)
        block = jnp.where(rows_of((MIG, 256)) < live, block, 0.0).astype(BF16)
        keyval_out[k] = block
        keyval.append(block)

    halves = []
    for h in range(2):
        span = slice(h * HEAD_DIM, (h + 1) * HEAD_DIM)
        scores = score(take(0, h), keyval[0][:, span])
        weights, weight_own = weigh(scores, own_score(h), lanes_of((8, MIG)) < live)
        migrated = jnp.dot(weights, keyval[1][:, span], preferred_element_type=F32)
        migrated = migrated + weight_own * take(2, h).astype(F32)
        halves.append(jnp.where(token < 4, resident[h], migrated))
    mixed_all[rep] = jnp.concatenate(halves, axis=1).astype(BF16).astype(F32)

    def send_mixed(peer):
        pltpu.make_async_remote_copy(
            src_ref=mixed_all.at[rep],
            dst_ref=mixed_all.at[rep],
            send_sem=mixed_sems.at[0],
            recv_sem=mixed_sems.at[1],
            device_id=(peer, head),
            device_id_type=MESH,
        ).start()

    all_peers(REP, rep, send_mixed)
    row, col = rows_of((ROWS, 128)), lanes_of((ROWS, 128))
    pack_rows = jnp.where((row // NQ) * 8 + lax.rem(row, NQ) == col, 1.0, 0.0).astype(BF16)
    loads[3].wait()
    wait_bytes(mixed_all.at[pl.ds(0, REP - 1)], mixed_sems.at[1])
    every = mixed_all[...].reshape(128, 256).astype(BF16)
    every = jnp.dot(pack_rows, every, preferred_element_type=F32).astype(BF16)
    update = jnp.dot(every, w_out[...], preferred_element_type=F32).astype(BF16)
    for i in range(5):
        for j in range(6):
            upd_send[i * 6 + j] = update[i * 16 : i * 16 + 16, j * 128 : j * 128 + 128]
    for i in range(30, 32):
        upd_send[i] = jnp.zeros((16, 128), BF16)
    upd_recv[head] = upd_send[head]

    def send_update(peer):
        pltpu.make_async_remote_copy(
            src_ref=upd_send.at[peer],
            dst_ref=upd_recv.at[head],
            send_sem=upd_sems.at[0],
            recv_sem=upd_sems.at[1],
            device_id=(rep, peer),
            device_id_type=MESH,
        ).start()

    all_peers(HEAD, head, send_update)
    wait_bytes(upd_recv.at[pl.ds(0, HEAD - 1)], upd_sems.at[1])
    final[head] = jnp.sum(upd_recv[...].astype(F32), axis=0).astype(BF16)

    def send_final(peer):
        pltpu.make_async_remote_copy(
            src_ref=final.at[head],
            dst_ref=final.at[head],
            send_sem=final_sems.at[0],
            recv_sem=final_sems.at[1],
            device_id=(rep, peer),
            device_id_type=MESH,
        ).start()

    all_peers(HEAD, head, send_final)
    wait_bytes(final.at[pl.ds(0, HEAD - 1)], final_sems.at[1])
    for i in range(5):
        for j in range(6):
            update_out[i * 16 : i * 16 + 16, j * 128 : j * 128 + 128] = final[i * 6 + j]

    for copy in sent:
        copy.wait_send()
    wait_bytes(stats.at[pl.ds(0, REP - 1)], stats_sems.at[0])
    wait_bytes(step_send.at[pl.ds(0, REP - 1)], step_sems.at[0])
    wait_bytes(mixed_all.at[pl.ds(0, REP - 1)], mixed_sems.at[0])
    wait_bytes(upd_send.at[pl.ds(0, HEAD - 1)], upd_sems.at[0])
    wait_bytes(final.at[pl.ds(0, HEAD - 1)], final_sems.at[0])


def on_device(
    step_hidden,
    paused_hidden,
    ln_gain,
    ln_bias,
    w_query,
    w_keyval,
    w_out,
    cache,
    cache_lengths,
    partner,
    paused_count,
):
    vmem = pl.BlockSpec(memory_space=pltpu.VMEM)
    smem = pl.BlockSpec(memory_space=pltpu.SMEM)
    anywhere = pl.BlockSpec(memory_space=pl.ANY)
    dma = pltpu.SemaphoreType.DMA
    keyval, update = pl.pallas_call(
        kernel,
        out_shape=(
            jax.ShapeDtypeStruct((2, MIG, 256), BF16),
            jax.ShapeDtypeStruct((ROWS, FEATS), BF16),
        ),
        in_specs=[smem] * 3 + [vmem] * 4 + [anywhere] * 4,
        out_specs=[vmem] * 2,
        scratch_shapes=[
            pltpu.VMEM((FEATS, 768), BF16),
            pltpu.VMEM((256, FEATS), BF16),
            pltpu.VMEM((4, 2, 512, 256), BF16),
            pltpu.VMEM((REP, 8, 128), F32),
            pltpu.VMEM((HEAD, 64, FEATS), BF16),
            pltpu.VMEM((REP, MIG, 512), F32),
            pltpu.VMEM((REP, 8, FEATS), F32),
            pltpu.VMEM((REP, 8, FEATS), F32),
            pltpu.VMEM((2, 2, 4, 2 * MIG, 256), BF16),
            pltpu.VMEM((2, 2, 4, 2 * MIG, 256), BF16),
            pltpu.VMEM((2, MIG, 256), BF16),
            pltpu.VMEM((2, MIG, 256), BF16),
            pltpu.VMEM((REP, 8, 256), F32),
            pltpu.VMEM((HEAD, 16, 128), BF16),
            pltpu.VMEM((HEAD, 16, 128), BF16),
            pltpu.VMEM((HEAD, 16, 128), BF16),
            dma((4,)),
            dma((2,)),
            dma((32,)),
            dma((HEAD,)),
            dma((2,)),
            dma((2, 2, 4)),
            dma((2, 2, 4)),
            dma((2,)),
            dma((2,)),
            dma((2,)),
            dma((2,)),
            dma((2,)),
        ],
        compiler_params=pltpu.CompilerParams(
            collective_id=0, has_side_effects=True, vmem_limit_bytes=40 * 1024 * 1024
        ),
        name="sublayer",
    )(
        partner,
        paused_count,
        cache_lengths,
        step_hidden,
        paused_hidden,
        ln_gain.reshape(1, -1),
        ln_bias.reshape(1, -1),
        w_query,
        w_keyval.reshape(-1, 512),
        w_out,
        cache,
    )
    return jnp.transpose(keyval, (1, 0, 2)), update


def solution(mesh):
    in_specs = (
        P(None, "rep"),
        P("head", "rep"),
        P("rep"),
        P("rep"),
        P("rep", "head"),
        P("rep", None, "head"),
        P("head", "rep"),
        P("rep", None, None, "head"),
        P("rep"),
        P(),
        P(),
    )
    out_specs = (P("rep", None, "head"), P(None, "rep"))
    return jax.shard_map(
        on_device, mesh=mesh, in_specs=in_specs, out_specs=out_specs, check_vma=False
    )
```

time: 461 us -> 109 us (0.24)
  blocking collectives: 248 us -> 0 us
  waiting for transfers between devices: 146 us -> 0 us
  Pallas kernels: 0 us -> 97 us
  other arithmetic: 17 us -> 0 us
  between operations: 16.8 us -> 0.66 us
  matrix products: 8.32 us -> 0 us
  local copies, waits for them, and re-layouts: 19.6 us -> 11.4 us
    psum x3 -> x0, blocking collectives: 224 us -> none  [the longest x1 144 us: on_device(): attention_update = lax.psum(partial_update, 'head').astype(jnp.bfloat16)]
    pallas_call x0 -> x1, Pallas kernels: none -> 97 us  [on_device(): pl.pallas_call(kernel, out_shape=(jax.ShapeDtypeStruct((2, MIG, 256), BF1...]
    all_gather x1 -> x0, waiting for transfers between devices: 73.5 us -> none  [on_device(): gathered = lax.all_gather(normed_paused, 'head', axis=0, tiled=True)]
    reduce_scatter x1 -> x0, waiting for transfers between devices: 72.7 us -> none  [on_device(): lax.psum_scatter(jnp.einsum('nd,dkw->nkw', picked, w_keyval, preferred_el...]
    all_gather x1 -> x0, blocking collectives: 24.8 us -> none  [on_device(): lax.all_gather(mixed, 'rep', axis=0, tiled=True)]
    gather x1 -> x0, local copies, waits for them, and re-layouts: 9.14 us -> none  [on_device(): picked = jnp.take(gathered, source, axis=0)]
    dot_general x8 -> x0, matrix products: 8.32 us -> none  [the longest x1 3.53 us: on_device(): jnp.einsum('nd,dkw->nkw', picked, w_keyval, preferred_element_type=jnp.fl...]
    unnamed x17 -> x19, local copies, waits for them, and re-layouts: 2.08 us -> 10 us
  transfers between devices with their start and end apart: 2 -> 0, of which waited for: 2 -> 0; matrix products, arithmetic and copies ran while one was open for 5% -> 0% of each run, Pallas kernels for 0% -> 0%
where the time goes in v1:
time: 109 us
  Pallas kernels  97 us (89%)
  local copies, waits for them, and re-layouts  11.4 us (10%)
    pallas_call x1, Pallas kernels, on_device(): pl.pallas_call(kernel, out_shape=(jax.ShapeDtypeStruct((2, MIG, 256), BF1...  97 us
    unnamed x19, local copies, waits for them, and re-layouts  10 us

profile of v1, /device:TPU:1, one launch (start us, length us, event | category | flops | bytes accessed | tf_op | source)
XLA Modules:
  0.0 109.1 jit_solution(13360910247336123918)
XLA Ops:
  0.6 0.7 reshape.13.gain_ref
  1.3 0.7 reshape.14.bias_ref
  2.0 1.3 %copy.14 = bf16[96,8,2,256]{3,1,2,0:T(8,128)(2,1)S(1)} copy(bf16[96,8,2,256]{3,2,1,0:T(2,128)(2,1)} %bitcast.5) | data formatting | bytes 1572864
  3.3 0.0 copy-start
  3.3 1.6 %copy-done = bf16[4,2,512,256]{3,2,1,0:T(8,128)(2,1)S(1)} copy-done((bf16[4,2,512,256]{3,2,1,0:T(8,128)(2,1)S(1)}, bf16[4,2,512,256]{3,2,1,0:T(8,128)(2,1)}, u32[]{:S(2)}) %copy-start) | copy-done | bytes 2097176
  4.9 0.0 copy-start.1
  4.9 1.0 copy-done.1
  5.9 0.0 copy-start.2
  5.9 1.0 copy-done.2
  6.9 0.0 copy-start.3
  6.9 0.9 copy-done.3
  7.8 0.0 copy-start.4
  7.8 0.9 copy-done.4
  8.7 0.0 copy-start.5
  8.7 0.7 copy-done.5
  9.3 0.0 copy-start.6
  9.3 0.7 copy-done.6
  10.0 0.0 copy-start.7
  10.0 0.7 copy-done.7
  10.7 97.0 %sublayer.1 = (bf16[2,112,256]{2,1,0:T(8,128)(2,1)S(1)}, bf16[80,768]{1,0:T(8,128)(2,1)S(1)}) custom-call(s32[16]{0:T(128)S(1)} %copy-done.5, s32[16]{0:T(128)S(1)} %copy-done.6, s32[4]{0:T(128)S(1)} %copy-done.7, bf16[80,768]{1,0:T(8,128)(2,1)S(1)} %copy-done.3, bf16[56,768]{1,0:T(8,128)(2,1)S(1)} %copy-done.4, f32[1,768]{1,0:T(1,128)S(1)} %reshape.13.gain_ref, ...), custom_call_target="tpu_custom_call" | custom-call | tf_op jit(solution)/shard_map/sublayer/pallas_call | solution.py:475
  107.7 0.7 copy.13
  108.4 0.6 copy.16
Async XLA Ops:
  3.3 1.6 %copy-start = (bf16[4,2,512,256]{3,2,1,0:T(8,128)(2,1)S(1)}, bf16[4,2,512,256]{3,2,1,0:T(8,128)(2,1)}, u32[]{:S(2)}) copy-start(bf16[4,2,512,256]{3,2,1,0:T(8,128)(2,1)} %cache_hbm.1) | copy-start | bytes 6291460
  4.9 1.0 copy-start.1
  5.9 1.0 copy-start.2
  6.9 0.9 copy-start.3
  7.8 0.9 copy-start.4
  8.7 0.7 copy-start.5
  9.3 0.7 copy-start.6
  10.0 0.7 copy-start.7

commit v2 on v0

v2 whole, which is shorter than its diff:
```python
import math

import jax
import jax.numpy as jnp
from jax import lax
from jax.experimental import pallas as pl
from jax.experimental.pallas import tpu as pltpu
from jax.sharding import PartitionSpec as P

D = 12288
HEAD_DIM = 128
MIG = 112
MESH = pl.DeviceIdType.MESH
F32 = jnp.float32
BF16 = jnp.bfloat16

REP = 16
HEAD = 32
FEATS = D // REP
HALF = MIG // 2
PIECE = 32
KEEP = (32, 24)
ROWS = 80
NQ = 5
FACTOR = 1.0 / math.sqrt(HEAD_DIM)


def rows_of(shape):
    return lax.broadcasted_iota(jnp.int32, shape, len(shape) - 2)


def lanes_of(shape):
    return lax.broadcasted_iota(jnp.int32, shape, len(shape) - 1)


def wait_bytes(ref, sem):
    pltpu.make_async_copy(ref, ref, sem).wait()


def push(src, dst, sems, device_id):
    pltpu.make_async_remote_copy(
        src_ref=src,
        dst_ref=dst,
        send_sem=sems.at[0],
        recv_sem=sems.at[1],
        device_id=device_id,
        device_id_type=MESH,
    ).start()


def kernel(
    partner_hbm,
    count_hbm,
    lengths_hbm,
    step_hbm,
    paused_hbm,
    gain_hbm,
    bias_hbm,
    w_query_hbm,
    w_keyval_hbm,
    w_out_hbm,
    cache_hbm,
    keyval_out,
    update_out,
    partner,
    paused_count,
    lengths,
    step_ref,
    paused_ref,
    gain_ref,
    bias_ref,
    w_pairs,
    w_split,
    w_all,
    w_out,
    cache,
    stats,
    stat_all,
    gathered,
    part0,
    part1,
    step_send,
    step_recv,
    ring_send0,
    ring_send1,
    ring_recv0,
    ring_recv1,
    pair_send0,
    pair_send1,
    pair_recv0,
    pair_recv1,
    mixed_res,
    mixed_mig,
    res_swap,
    res_z,
    res_x,
    res_fin,
    mig_swap,
    mig_z,
    mig_x,
    mig_fin,
    load_sem,
    stats_sems,
    statz_sems,
    statx_sems,
    ag_send,
    ag_recv,
    row_send,
    row_recv,
    step_sems,
    ring_ssem,
    ring_rsem,
    pair_ssem,
    pair_rsem,
    mres_sems,
    mmig_sems,
    res_sems,
    mig_sems,
):
    rep = lax.axis_index("rep")
    head = lax.axis_index("head")
    y, zl = rep // 2, lax.rem(rep, 2)
    core = lax.rem(head, 2)
    chip = head // 2
    zh, x = chip // 4, lax.rem(chip, 4)

    def at_head(jz, jx, c):
        return (rep, (lax.rem(zh + jz + 4, 4) * 4 + lax.rem(x + jx + 4, 4)) * 2 + c)

    z_peers = [at_head(j, 0, core) for j in (2, 1, 3)]
    x_peers = [at_head(0, j, core) for j in (2, 1, 3)]
    cross_peers = [at_head(0, j, 1 - core) for j in (2, 1, 3)]
    twin = at_head(0, 0, 1 - core)

    sources = [
        (paused_hbm, paused_ref),
        (step_hbm, step_ref),
        (gain_hbm, gain_ref),
        (bias_hbm, bias_ref),
        (w_keyval_hbm, w_pairs),
        (w_query_hbm, w_all.at[:, pl.ds(0, 256)]),
        (partner_hbm, partner),
        (count_hbm, paused_count),
        (lengths_hbm, lengths),
        (cache_hbm, cache),
        (w_out_hbm, w_out),
    ]
    loads = [
        pltpu.make_async_copy(src, dst, load_sem.at[i]) for i, (src, dst) in enumerate(sources)
    ]
    loads[0].start()

    barrier = pltpu.get_barrier_semaphore()
    for peer in z_peers + x_peers + cross_peers + [twin]:
        pl.semaphore_signal(barrier, inc=1, device_id=peer, device_id_type=MESH)

    def greet_rep(d, carry):
        pl.semaphore_signal(
            barrier, inc=1, device_id=(lax.rem(rep + d, REP), head), device_id_type=MESH
        )
        return carry

    lax.fori_loop(1, REP, greet_rep, 0)
    for load in loads[1:]:
        load.start()

    def to_rep(send):
        def body(d, carry):
            send(lax.rem(rep + d, REP))
            return carry

        lax.fori_loop(1, REP, body, 0)

    own_slot = core * 16 + chip
    loads[0].wait()
    own_rows = paused_ref[...].astype(F32)
    gathered[0, own_slot] = own_rows[:PIECE].astype(BF16)
    gathered[1, own_slot] = jnp.concatenate(
        [own_rows[PIECE:], jnp.zeros((2 * PIECE - HALF, FEATS), F32)], axis=0
    ).astype(BF16)

    pl.semaphore_wait(barrier, REP - 1 + 10)

    def slot_of(jz, jx):
        return core * 16 + lax.rem(zh + jz + 4, 4) * 4 + lax.rem(x + jx + 4, 4)

    def pass_on(p, jz, jx, tz, tx):
        block = gathered.at[p, slot_of(jz, jx)]
        pltpu.make_async_remote_copy(
            src_ref=block,
            dst_ref=block,
            send_sem=ag_send.at[p],
            recv_sem=ag_recv.at[p, slot_of(jz, jx)],
            device_id=at_head(tz, tx, core),
            device_id_type=MESH,
        ).start()

    def row_on(p, jz):
        row = lax.rem(zh + jz + 4, 4)
        block = gathered.at[p, pl.ds(core * 16 + row * 4, 4)]
        pltpu.make_async_remote_copy(
            src_ref=block,
            dst_ref=block,
            send_sem=row_send.at[p],
            recv_sem=row_recv.at[p, row],
            device_id=twin,
            device_id_type=MESH,
        ).start()

    def own_on(p):
        pass_on(p, 0, 0, 1, 0)
        pass_on(p, 0, 0, -1, 0)
        pass_on(p, 0, 0, 0, 1)
        pass_on(p, 0, 0, 0, -1)

    def arrive(p, *places):
        for jz, jx in places:
            where = slot_of(jz, jx)
            wait_bytes(gathered.at[p, where], ag_recv.at[p, where])
            if jx == 0:
                if jz == -1:
                    pass_on(p, jz, jx, 1, 0)
                pass_on(p, jz, jx, 0, 1)
                pass_on(p, jz, jx, 0, -1)
            if jx == -1 and jz in (0, 2):
                pass_on(p, jz, jx, 0, 1)
            if jx == 1 and jz in (-1, 1):
                pass_on(p, jz, jx, 0, -1)
            if jx == 2:
                row_on(p, jz)

    own_on(0)
    own_on(1)

    def local_stats(wide):
        mean = jnp.sum(wide, axis=1, keepdims=True) / FEATS
        offset = wide - mean
        return mean, jnp.sum(offset * offset, axis=1, keepdims=True)

    def place(pair, lane, rows):
        lanes = lanes_of((rows, 128))
        block = jnp.where(lanes == lane, pair[0], jnp.where(lanes == lane + 1, pair[1], 0.0))
        return jnp.concatenate([block, jnp.zeros((128 - rows, 128), F32)], axis=0)

    loads[1].wait()
    packed = place(local_stats(step_ref[...].astype(F32)), 0, ROWS) + place(
        local_stats(own_rows), 2, HALF
    )
    stats[rep] = jnp.transpose(packed)[:8]
    to_rep(lambda peer: push(stats.at[rep], stats.at[rep], stats_sems, (peer, head)))

    for i in range(2, 9):
        loads[i].wait()

    def split(i, carry):
        wide = w_pairs[pl.ds(i * 32, 32)].reshape(64, 256).astype(F32)
        w_split[pl.ds(0, 64)] = wide[:, :128]
        w_split[pl.ds(64, 64)] = wide[:, 128:]
        for k in range(2):
            for j in range(2):
                start = 256 + k * 256 + j * 128
                w_all[pl.ds(i * 32, 32), start : start + 128] = w_split[
                    pl.ds(k + 64 * j, 32, stride=2), :
                ].astype(BF16)
        return carry

    lax.fori_loop(0, FEATS // 32, split, 0)

    arrive(0, (0, -1), (0, 1), (-1, 0), (1, 0))
    arrive(1, (0, -1), (0, 1), (-1, 0), (1, 0))

    wait_bytes(stats.at[pl.ds(0, REP - 1)], stats_sems.at[1])
    every = stats[...]
    mean = jnp.sum(every, axis=0) / REP
    away = every - mean[None]
    away = jnp.sum(away * away, axis=0)
    sums = mean * REP

    def scale_of(row):
        spread = (sums[row + 1 : row + 2] + FEATS * away[row : row + 1]) / D
        return lax.rsqrt(spread + 1e-05)

    lines = jnp.concatenate(
        [mean[0:1], scale_of(0), mean[2:3], scale_of(2), jnp.zeros((4, 128), F32)], axis=0
    )
    stat_slot = core * 16 + x * 4 + zh
    stat_all[stat_slot] = lines
    for peer in z_peers:
        push(stat_all.at[stat_slot], stat_all.at[stat_slot], statz_sems, peer)

    gain = gain_ref[...].reshape(1, FEATS)
    bias = bias_ref[...].reshape(1, FEATS)

    def normalize(wide, columns, lane):
        center = columns[:, lane : lane + 1]
        scale = columns[:, lane + 1 : lane + 2]
        return ((wide - center) * scale * gain + bias).astype(BF16)

    arrive(0, (2, 0), (0, 2), (-1, -1), (-1, 1), (1, -1), (1, 1))

    normed_step = normalize(step_ref[...].astype(F32), jnp.transpose(lines)[:ROWS], 0)
    row, col = rows_of((128, ROWS)), lanes_of((128, ROWS))
    spread_rows = jnp.where((row // 8) * NQ + lax.rem(row, 8) == col, 1.0, 0.0)
    spread_rows = jnp.where(lax.rem(row, 8) < NQ, spread_rows, 0.0).astype(BF16)
    padded_step = jnp.dot(spread_rows, normed_step, preferred_element_type=F32).astype(BF16)
    step_part = jnp.dot(padded_step, w_all[...], preferred_element_type=F32)
    step_send[...] = step_part.reshape(REP, 8, FEATS)
    step_recv[rep] = step_send[rep]

    wait_bytes(stat_all.at[pl.ds(0, 3)], statz_sems.at[1])
    stat_line = stat_all.at[pl.ds(core * 16 + x * 4, 4)]
    for peer in x_peers + cross_peers + [twin]:
        push(stat_line, stat_line, statx_sems, peer)

    to_rep(lambda peer: push(step_send.at[peer], step_recv.at[rep], step_sems, (peer, head)))

    arrive(1, (2, 0), (0, 2), (-1, -1), (-1, 1), (1, -1), (1, 1))
    arrive(0, (2, -1), (2, 1), (-1, 2), (1, 2), (2, 2))

    parts = (part0, part1)

    def project(p):
        def body(i, carry):
            rows = []
            for j in range(8):
                lines = stat_all[(i // 2) * 16 + (j % 4) * 4 + lax.rem(i, 2) * 2 + j // 4]
                columns = jnp.transpose(lines)[p * PIECE : (p + 1) * PIECE]
                rows.append(normalize(gathered[p, i * 8 + j].astype(F32), columns, 2))
            rows = jnp.concatenate(rows, axis=0)
            found = jnp.dot(rows, w_all[:, 256:], preferred_element_type=F32)
            found = found.reshape(8, PIECE, 512)
            parts[p][i // 2, pl.ds(lax.rem(i, 2) * 8, 8)] = found[:, : KEEP[p]]
            return carry

        for r in range(4):
            wait_bytes(gathered.at[p, pl.ds(0, 4)], row_recv.at[p, r])
        lax.fori_loop(0, 4, body, 0)

    ring_send, ring_recv = (ring_send0, ring_send1), (ring_recv0, ring_recv1)

    def own_part(p, to_y, k):
        blocks = []
        for z in range(2):
            group = partner[to_y * 2 + z]
            for c in range(2):
                blocks.append(parts[p][c, group, :, k * 256 : (k + 1) * 256])
        return jnp.concatenate(blocks, axis=0)

    def ring_step(p, s):
        for k in range(2):
            for way in range(2):
                steps = 4 if way == k else 3
                if s >= steps:
                    continue
                sign = 1 if way == 0 else -1
                here = (way * 2 + k) * 4 + s
                block = own_part(p, lax.rem(y + sign * (steps - s) + 8, 8), k)
                if s > 0:
                    wait_bytes(ring_recv[p].at[here - 1], ring_rsem.at[p, here - 1])
                    block = block + ring_recv[p][here - 1].astype(F32)
                ring_send[p][here] = block.astype(BF16)
                pltpu.make_async_remote_copy(
                    src_ref=ring_send[p].at[here],
                    dst_ref=ring_recv[p].at[here],
                    send_sem=ring_ssem.at[p, here],
                    recv_sem=ring_rsem.at[p, here],
                    device_id=(lax.rem(y + sign + 8, 8) * 2 + zl, head),
                    device_id_type=MESH,
                ).start()

    pair_send, pair_recv = (pair_send0, pair_send1), (pair_recv0, pair_recv1)

    def ring_end(p):
        totals = []
        for k in range(2):
            block = own_part(p, y, k)
            for way in range(2):
                last = (way * 2 + k) * 4 + (4 if way == k else 3) - 1
                wait_bytes(ring_recv[p].at[last], ring_rsem.at[p, last])
                block = block + ring_recv[p][last].astype(F32)
            low, high = block[: 2 * KEEP[p]], block[2 * KEEP[p] :]
            totals.append(jnp.where(zl == 0, low, high))
            pair_send[p][k] = jnp.where(zl == 0, high, low).astype(BF16)
            pltpu.make_async_remote_copy(
                src_ref=pair_send[p].at[k],
                dst_ref=pair_recv[p].at[k],
                send_sem=pair_ssem.at[p, k],
                recv_sem=pair_rsem.at[p, k],
                device_id=(y * 2 + 1 - zl, head),
                device_id_type=MESH,
            ).start()
        return totals

    def weigh(scores, own, valid):
        scores = jnp.where(valid, scores, -jnp.inf)
        top = jnp.maximum(jnp.max(scores, axis=1, keepdims=True), own)
        expo = jnp.exp(scores - top)
        expo_own = jnp.exp(own - top)
        total = jnp.sum(expo, axis=1, keepdims=True) + expo_own
        return (expo / total).astype(BF16), (expo_own / total).astype(BF16).astype(F32)

    def score(query, keys):
        dims = (((1,), (1,)), ((), ()))
        return lax.dot_general(query, keys, dims, preferred_element_type=F32) * FACTOR

    def take(part, h):
        start = part * 256 + h * HEAD_DIM
        return step_qkv[:, start : start + HEAD_DIM]

    def own_score(h):
        products = take(0, h).astype(F32) * take(1, h).astype(F32)
        return jnp.sum(products, axis=1, keepdims=True) * FACTOR

    def swap_halves(update, swap, sems):
        left, right = update[:, :384], update[:, 384:]
        swap[0] = jnp.where(core == 0, right, left).astype(BF16)
        push(swap.at[0], swap.at[1], sems.at[0], twin)
        return jnp.where(core == 0, left, right)

    def spread(block, buffer, me, peers, sems):
        buffer[me] = block.astype(BF16)
        for peer in peers:
            push(buffer.at[me], buffer.at[me], sems, peer)

    def sum_over_z(mine, swap, buffer, sems):
        wait_bytes(swap.at[1], sems.at[0, 1])
        spread(mine + swap[1].astype(F32), buffer, zh, z_peers, sems.at[1])

    def sum_over_x(buffer, wide, sems):
        wait_bytes(buffer.at[pl.ds(0, 3)], sems.at[1, 1])
        spread(jnp.sum(buffer[...].astype(F32), axis=0), wide, x, x_peers, sems.at[2])

    def join(buffer, fin, sems):
        wait_bytes(buffer.at[pl.ds(0, 3)], sems.at[2, 1])
        fin[core] = jnp.sum(buffer[...].astype(F32), axis=0).astype(BF16)
        push(fin.at[core], fin.at[core], sems.at[3], twin)

    def joined(fin, sems):
        wait_bytes(fin.at[0], sems.at[3, 1])
        return jnp.concatenate([fin[0], fin[1]], axis=1)

    def drained(swap, buffer, wide, fin, sems):
        wait_bytes(swap.at[0], sems.at[0, 0])
        wait_bytes(buffer.at[pl.ds(0, 3)], sems.at[1, 0])
        wait_bytes(wide.at[pl.ds(0, 3)], sems.at[2, 0])
        wait_bytes(fin.at[0], sems.at[3, 0])

    wait_bytes(stat_all.at[pl.ds(0, 28)], statx_sems.at[1])
    project(0)
    ring_step(0, 0)
    arrive(1, (2, -1), (2, 1), (-1, 2), (1, 2), (2, 2))
    ring_step(0, 1)
    project(1)
    ring_step(1, 0)
    ring_step(0, 2)

    wait_bytes(step_recv.at[pl.ds(0, REP - 1)], step_sems.at[1])
    step_qkv = jnp.sum(step_recv[...], axis=0).astype(BF16)
    loads[9].wait()
    row = rows_of((8, 512))
    limit = jnp.zeros((8, 512), jnp.int32)
    for b in range(4):
        limit = jnp.where(row == b, lengths[b], limit)
    valid = lanes_of((8, 512)) < limit
    token = rows_of((8, HEAD_DIM))
    halves = []
    for h in range(2):
        span = slice(h * HEAD_DIM, (h + 1) * HEAD_DIM)
        scores = jnp.zeros((8, 512), F32)
        for b in range(4):
            scores = jnp.where(row == b, score(take(0, h), cache[b, 0, :, span]), scores)
        weights, weight_own = weigh(scores, own_score(h), valid)
        mixed = jnp.zeros((8, HEAD_DIM), F32)
        for b in range(4):
            found = jnp.dot(weights, cache[b, 1, :, span], preferred_element_type=F32)
            mixed = jnp.where(token == b, found, mixed)
        halves.append(mixed + weight_own * take(2, h).astype(F32))
    mixed_res[rep] = jnp.concatenate(halves, axis=1).astype(BF16).astype(F32)
    to_rep(lambda peer: push(mixed_res.at[rep], mixed_res.at[rep], mres_sems, (peer, head)))

    ring_step(1, 1)
    ring_step(0, 3)

    wait_bytes(mixed_res.at[pl.ds(0, REP - 1)], mres_sems.at[1])
    loads[10].wait()
    row, col = rows_of((64, 128)), lanes_of((64, 128))
    pack_rows = jnp.where((row // 4) * 8 + lax.rem(row, 4) == col, 1.0, 0.0).astype(BF16)
    every = mixed_res[...].reshape(128, 256).astype(BF16)
    every = jnp.dot(pack_rows, every, preferred_element_type=F32).astype(BF16)
    update = jnp.dot(every, w_out[...], preferred_element_type=F32)
    mine = swap_halves(update, res_swap, res_sems)

    ring_step(1, 2)
    totals0 = ring_end(0)
    sum_over_z(mine, res_swap, res_z, res_sems)
    ring_step(1, 3)
    sum_over_x(res_z, res_x, res_sems)
    totals1 = ring_end(1)
    join(res_x, res_fin, res_sems)

    live = paused_count[partner[rep]]
    keyval = []
    for k in range(2):
        blocks = []
        for p, totals in enumerate((totals0, totals1)):
            wait_bytes(pair_recv[p].at[k], pair_rsem.at[p, k])
            blocks.append(totals[k] + pair_recv[p][k].astype(F32))
        first, second = blocks
        block = jnp.concatenate(
            [first[: KEEP[0]], second[: KEEP[1]], first[KEEP[0] :], second[KEEP[1] :]], axis=0
        )
        block = jnp.where(rows_of((MIG, 256)) < live, block, 0.0).astype(BF16)
        keyval_out[k] = block
        keyval.append(block)

    halves = []
    for h in range(2):
        span = slice(h * HEAD_DIM, (h + 1) * HEAD_DIM)
        scores = score(take(0, h), keyval[0][:, span])
        weights, weight_own = weigh(scores, own_score(h), lanes_of((8, MIG)) < live)
        migrated = jnp.dot(weights, keyval[1][:, span], preferred_element_type=F32)
        migrated = migrated + weight_own * take(2, h).astype(F32)
        halves.append(migrated[4:5])
    halves.append(jnp.zeros((6, HEAD_DIM), F32))
    mixed_mig[rep] = jnp.concatenate(halves, axis=0).astype(BF16).astype(F32)
    to_rep(lambda peer: push(mixed_mig.at[rep], mixed_mig.at[rep], mmig_sems, (peer, head)))

    resident = joined(res_fin, res_sems)
    row, col = rows_of((ROWS, 64)), lanes_of((ROWS, 64))
    spread_rows = jnp.where((row // NQ) * 4 + lax.rem(row, NQ) == col, 1.0, 0.0)
    spread_rows = jnp.where(lax.rem(row, NQ) < 4, spread_rows, 0.0).astype(BF16)
    resident = jnp.dot(spread_rows, resident, preferred_element_type=F32)

    wait_bytes(mixed_mig.at[pl.ds(0, REP - 1)], mmig_sems.at[1])
    every = mixed_mig[...].reshape(128, HEAD_DIM).astype(BF16)
    row, col = rows_of((16, 128)), lanes_of((16, 128))
    update = jnp.zeros((16, FEATS), F32)
    for h in range(2):
        pick = jnp.where(row * 8 + h == col, 1.0, 0.0).astype(BF16)
        rows = jnp.dot(pick, every, preferred_element_type=F32).astype(BF16)
        update = update + jnp.dot(
            rows, w_out[h * HEAD_DIM : (h + 1) * HEAD_DIM, :], preferred_element_type=F32
        )
    mine = swap_halves(update, mig_swap, mig_sems)
    sum_over_z(mine, mig_swap, mig_z, mig_sems)
    sum_over_x(mig_z, mig_x, mig_sems)
    join(mig_x, mig_fin, mig_sems)
    migrated = joined(mig_fin, mig_sems)
    row, col = rows_of((ROWS, 16)), lanes_of((ROWS, 16))
    spread_rows = jnp.where(col * NQ + 4 == row, 1.0, 0.0).astype(BF16)
    migrated = jnp.dot(spread_rows, migrated, preferred_element_type=F32)
    update_out[...] = (resident + migrated).astype(BF16)

    wait_bytes(stats.at[pl.ds(0, REP - 1)], stats_sems.at[0])
    wait_bytes(stat_all.at[pl.ds(0, 3)], statz_sems.at[0])
    wait_bytes(stat_all.at[pl.ds(0, 28)], statx_sems.at[0])
    wait_bytes(step_send.at[pl.ds(0, REP - 1)], step_sems.at[0])
    wait_bytes(mixed_res.at[pl.ds(0, REP - 1)], mres_sems.at[0])
    wait_bytes(mixed_mig.at[pl.ds(0, REP - 1)], mmig_sems.at[0])
    for p in range(2):
        wait_bytes(gathered.at[p, pl.ds(0, 15)], ag_send.at[p])
        wait_bytes(gathered.at[p, pl.ds(0, 16)], row_send.at[p])
        for k in range(2):
            wait_bytes(pair_send[p].at[k], pair_ssem.at[p, k])
            for way in range(2):
                for s in range(4 if way == k else 3):
                    here = (way * 2 + k) * 4 + s
                    wait_bytes(ring_send[p].at[here], ring_ssem.at[p, here])
    drained(res_swap, res_z, res_x, res_fin, res_sems)
    drained(mig_swap, mig_z, mig_x, mig_fin, mig_sems)


def on_device(
    step_hidden,
    paused_hidden,
    ln_gain,
    ln_bias,
    w_query,
    w_keyval,
    w_out,
    cache,
    cache_lengths,
    partner,
    paused_count,
):
    vmem = pl.BlockSpec(memory_space=pltpu.VMEM)
    anywhere = pl.BlockSpec(memory_space=pltpu.HBM)
    dma = pltpu.SemaphoreType.DMA
    ring = [pltpu.VMEM((16, 4 * keep, 256), BF16) for keep in KEEP]
    pair = [pltpu.VMEM((2, 2 * keep, 256), BF16) for keep in KEEP]

    def reduction(rows):
        return [
            pltpu.VMEM((2, rows, 384), BF16),
            pltpu.VMEM((4, rows, 384), BF16),
            pltpu.VMEM((4, rows, 384), BF16),
            pltpu.VMEM((2, rows, 384), BF16),
        ]

    keyval, update = pl.pallas_call(
        kernel,
        out_shape=(
            jax.ShapeDtypeStruct((2, MIG, 256), BF16),
            jax.ShapeDtypeStruct((ROWS, FEATS), BF16),
        ),
        in_specs=[anywhere] * 11,
        out_specs=[vmem] * 2,
        scratch_shapes=[
            pltpu.SMEM((REP,), jnp.int32),
            pltpu.SMEM((REP,), jnp.int32),
            pltpu.SMEM((4,), jnp.int32),
            pltpu.VMEM((ROWS, FEATS), BF16),
            pltpu.VMEM((HALF, FEATS), BF16),
            pltpu.VMEM((FEATS,), F32),
            pltpu.VMEM((FEATS,), F32),
            pltpu.VMEM((FEATS, 2, 256), BF16),
            pltpu.VMEM((128, 128), F32),
            pltpu.VMEM((FEATS, 768), BF16),
            pltpu.VMEM((256, FEATS), BF16),
            pltpu.VMEM((4, 2, 512, 256), BF16),
            pltpu.VMEM((REP, 8, 128), F32),
            pltpu.VMEM((HEAD, 8, 128), F32),
            pltpu.VMEM((2, HEAD, PIECE, FEATS), BF16),
            pltpu.VMEM((2, REP, KEEP[0], 512), F32),
            pltpu.VMEM((2, REP, KEEP[1], 512), F32),
            pltpu.VMEM((REP, 8, FEATS), F32),
            pltpu.VMEM((REP, 8, FEATS), F32),
        ]
        + ring * 2
        + pair * 2
        + [pltpu.VMEM((REP, 8, 256), F32), pltpu.VMEM((REP, 8, 128), F32)]
        + reduction(64)
        + reduction(16)
        + [
            dma((11,)),
            dma((2,)),
            dma((2,)),
            dma((2,)),
            dma((2,)),
            dma((2, HEAD)),
            dma((2,)),
            dma((2, 4)),
            dma((2,)),
            dma((2, 16)),
            dma((2, 16)),
            dma((2, 2)),
            dma((2, 2)),
            dma((2,)),
            dma((2,)),
            dma((4, 2)),
            dma((4, 2)),
        ],
        compiler_params=pltpu.CompilerParams(
            collective_id=0, has_side_effects=True, vmem_limit_bytes=60 * 1024 * 1024
        ),
        name="sublayer",
    )(
        partner,
        paused_count,
        cache_lengths,
        step_hidden,
        paused_hidden,
        ln_gain,
        ln_bias,
        w_query,
        w_keyval,
        w_out,
        cache,
    )
    return jnp.transpose(keyval, (1, 0, 2)), update


def solution(mesh):
    in_specs = (
        P(None, "rep"),
        P("head", "rep"),
        P("rep"),
        P("rep"),
        P("rep", "head"),
        P("rep", None, "head"),
        P("head", "rep"),
        P("rep", None, None, "head"),
        P("rep"),
        P(),
        P(),
    )
    out_specs = (P("rep", None, "head"), P(None, "rep"))
    return jax.shard_map(
        on_device, mesh=mesh, in_specs=in_specs, out_specs=out_specs, check_vma=False
    )
```

time: 461 us -> 92.8 us (0.20)
  blocking collectives: 248 us -> 0 us
  waiting for transfers between devices: 146 us -> 0 us
  Pallas kernels: 0 us -> 88.8 us
  other arithmetic: 17 us -> 0 us
  local copies, waits for them, and re-layouts: 19.6 us -> 3.19 us
  between operations: 16.8 us -> 0.64 us
  matrix products: 8.32 us -> 0 us
    psum x3 -> x0, blocking collectives: 224 us -> none  [the longest x1 144 us: on_device(): attention_update = lax.psum(partial_update, 'head').astype(jnp.bfloat16)]
    pallas_call x0 -> x1, Pallas kernels: none -> 88.8 us  [on_device(): pl.pallas_call(kernel, out_shape=(jax.ShapeDtypeStruct((2, MIG, 256), BF1...]
    all_gather x1 -> x0, waiting for transfers between devices: 73.5 us -> none  [on_device(): gathered = lax.all_gather(normed_paused, 'head', axis=0, tiled=True)]
    reduce_scatter x1 -> x0, waiting for transfers between devices: 72.7 us -> none  [on_device(): lax.psum_scatter(jnp.einsum('nd,dkw->nkw', picked, w_keyval, preferred_el...]
    all_gather x1 -> x0, blocking collectives: 24.8 us -> none  [on_device(): lax.all_gather(mixed, 'rep', axis=0, tiled=True)]
    gather x1 -> x0, local copies, waits for them, and re-layouts: 9.14 us -> none  [on_device(): picked = jnp.take(gathered, source, axis=0)]
    dot_general x8 -> x0, matrix products: 8.32 us -> none  [the longest x1 3.53 us: on_device(): jnp.einsum('nd,dkw->nkw', picked, w_keyval, preferred_element_type=jnp.fl...]
    and x1 -> x0, other arithmetic: 5.43 us -> none  [on_device(): picked = jnp.take(gathered, source, axis=0)]
  transfers between devices with their start and end apart: 2 -> 0, of which waited for: 2 -> 0; matrix products, arithmetic and copies ran while one was open for 5% -> 0% of each run, Pallas kernels for 0% -> 0%
where the time goes in v2:
time: 92.8 us; the launch traced here: 92.7 us
  Pallas kernels  88.8 us (96%)
  local copies, waits for them, and re-layouts  3.19 us (3%)
    pallas_call x1, Pallas kernels, on_device(): pl.pallas_call(kernel, out_shape=(jax.ShapeDtypeStruct((2, MIG, 256), BF1...  88.8 us
    unnamed x2, local copies, waits for them, and re-layouts  3.19 us

profile of v2, /device:TPU:1, one launch (start us, length us, event | category | flops | bytes accessed | tf_op | source)
XLA Modules:
  0.0 92.7 jit_solution(1895077377497601820)
XLA Ops:
  0.6 88.8 %sublayer.1 = (bf16[2,112,256]{2,1,0:T(8,128)(2,1)}, bf16[80,768]{1,0:T(8,128)(2,1)}) custom-call(s32[16]{0:T(128)} %partner_hbm.1, s32[16]{0:T(128)} %count_hbm.1, s32[4]{0:T(128)} %lengths_hbm.1, bf16[80,768]{1,0:T(8,128)(2,1)} %step_hbm.1, bf16[56,768]{1,0:T(8,128)(2,1)} %paused_hbm.1, f32[768]{0:T(1024)} %gain_hbm.1, f32[768]{0:T(1024)} %bias_hbm.1, ...), custom_call_target="tpu_custom_call" | custom-call | tf_op jit(solution)/shard_map/sublayer/pallas_call | solution.py:600
  89.5 1.6 %copy.13 = bf16[112,2,256]{2,1,0:T(2,128)(2,1)} copy(bf16[112,2,256]{2,0,1:T(8,128)(2,1)} %bitcast.1) | data formatting | bytes 229376
  91.1 1.6 %copy.15 = bf16[80,768]{1,0:T(8,128)(2,1)} copy(bf16[80,768]{1,0:T(8,128)(2,1)} %get-tuple-element.11) | data formatting | bytes 245760

commit v3 on v2

--- a/solution.py
+++ b/solution.py
@@ -18,7 +18,6 @@
 HEAD = 32
 FEATS = D // REP
 HALF = MIG // 2
-PIECE = 32
 KEEP = (32, 24)
 ROWS = 80
 NQ = 5
@@ -76,7 +75,8 @@
     cache,
     stats,
     stat_all,
-    gathered,
+    gathered0,
+    gathered1,
     part0,
     part1,
     step_send,
@@ -171,12 +171,19 @@
 
         lax.fori_loop(1, REP, body, 0)
 
+    gathered = (gathered0, gathered1)
     own_slot = core * 16 + chip
     loads[0].wait()
     own_rows = paused_ref[...].astype(F32)
-    gathered[0, own_slot] = own_rows[:PIECE].astype(BF16)
-    gathered[1, own_slot] = jnp.concatenate(
-        [own_rows[PIECE:], jnp.zeros((2 * PIECE - HALF, FEATS), F32)], axis=0
+    gathered0[own_slot] = own_rows[: KEEP[0]].astype(BF16)
+    gathered1[own_slot] = jnp.concatenate(
+        [
+            own_rows[32:48, :384],
+            own_rows[32:48, 384:],
+            own_rows[48:56, :384],
+            own_rows[48:56, 384:],
+        ],
+        axis=0,
     ).astype(BF16)
 
     pl.semaphore_wait(barrier, REP - 1 + 10)
@@ -185,7 +192,7 @@
         return core * 16 + lax.rem(zh + jz + 4, 4) * 4 + lax.rem(x + jx + 4, 4)
 
     def pass_on(p, jz, jx, tz, tx):
-        block = gathered.at[p, slot_of(jz, jx)]
+        block = gathered[p].at[slot_of(jz, jx)]
         pltpu.make_async_remote_copy(
             src_ref=block,
             dst_ref=block,
@@ -197,7 +204,7 @@
 
     def row_on(p, jz):
         row = lax.rem(zh + jz + 4, 4)
-        block = gathered.at[p, pl.ds(core * 16 + row * 4, 4)]
+        block = gathered[p].at[pl.ds(core * 16 + row * 4, 4)]
         pltpu.make_async_remote_copy(
             src_ref=block,
             dst_ref=block,
@@ -216,7 +223,7 @@
     def arrive(p, *places):
         for jz, jx in places:
             where = slot_of(jz, jx)
-            wait_bytes(gathered.at[p, where], ag_recv.at[p, where])
+            wait_bytes(gathered[p].at[where], ag_recv.at[p, where])
             if jx == 0:
                 if jz == -1:
                     pass_on(p, jz, jx, 1, 0)
@@ -297,6 +304,11 @@
         return ((wide - center) * scale * gain + bias).astype(BF16)
 
     arrive(0, (2, 0), (0, 2), (-1, -1), (-1, 1), (1, -1), (1, 1))
+    arrive(1, (2, 0), (0, 2), (-1, -1), (-1, 1), (1, -1), (1, 1))
+    wait_bytes(stat_all.at[pl.ds(0, 3)], statz_sems.at[1])
+    stat_line = stat_all.at[pl.ds(core * 16 + x * 4, 4)]
+    for peer in x_peers + cross_peers + [twin]:
+        push(stat_line, stat_line, statx_sems, peer)
 
     normed_step = normalize(step_ref[...].astype(F32), jnp.transpose(lines)[:ROWS], 0)
     row, col = rows_of((128, ROWS)), lanes_of((128, ROWS))
@@ -307,15 +319,10 @@
     step_send[...] = step_part.reshape(REP, 8, FEATS)
     step_recv[rep] = step_send[rep]
 
-    wait_bytes(stat_all.at[pl.ds(0, 3)], statz_sems.at[1])
-    stat_line = stat_all.at[pl.ds(core * 16 + x * 4, 4)]
-    for peer in x_peers + cross_peers + [twin]:
-        push(stat_line, stat_line, statx_sems, peer)
-
     to_rep(lambda peer: push(step_send.at[peer], step_recv.at[rep], step_sems, (peer, head)))
 
-    arrive(1, (2, 0), (0, 2), (-1, -1), (-1, 1), (1, -1), (1, 1))
     arrive(0, (2, -1), (2, 1), (-1, 2), (1, 2), (2, 2))
+    arrive(1, (2, -1), (2, 1))
 
     parts = (part0, part1)
 
@@ -324,16 +331,21 @@
             rows = []
             for j in range(8):
                 lines = stat_all[(i // 2) * 16 + (j % 4) * 4 + lax.rem(i, 2) * 2 + j // 4]
-                columns = jnp.transpose(lines)[p * PIECE : (p + 1) * PIECE]
-                rows.append(normalize(gathered[p, i * 8 + j].astype(F32), columns, 2))
-            rows = jnp.concatenate(rows, axis=0)
+                columns = jnp.transpose(lines)[p * KEEP[0] : p * KEEP[0] + KEEP[p]]
+                block = gathered[p][i * 8 + j].astype(F32)
+                if p == 1:
+                    left = jnp.concatenate([block[0:16], block[32:40]], axis=0)
+                    right = jnp.concatenate([block[16:32], block[40:48]], axis=0)
+                    block = jnp.concatenate([left, right], axis=1)
+                rows.append(normalize(block, columns, 2).astype(F32))
+            rows = jnp.concatenate(rows, axis=0).astype(BF16)
             found = jnp.dot(rows, w_all[:, 256:], preferred_element_type=F32)
-            found = found.reshape(8, PIECE, 512)
-            parts[p][i // 2, pl.ds(lax.rem(i, 2) * 8, 8)] = found[:, : KEEP[p]]
+            found = found.reshape(8, KEEP[p], 512)
+            parts[p][i // 2, pl.ds(lax.rem(i, 2) * 8, 8)] = found
             return carry
 
         for r in range(4):
-            wait_bytes(gathered.at[p, pl.ds(0, 4)], row_recv.at[p, r])
+            wait_bytes(gathered[p].at[pl.ds(0, 4)], row_recv.at[p, r])
         lax.fori_loop(0, 4, body, 0)
 
     ring_send, ring_recv = (ring_send0, ring_send1), (ring_recv0, ring_recv1)
@@ -448,38 +460,46 @@
     wait_bytes(stat_all.at[pl.ds(0, 28)], statx_sems.at[1])
     project(0)
     ring_step(0, 0)
-    arrive(1, (2, -1), (2, 1), (-1, 2), (1, 2), (2, 2))
+
+    wait_bytes(step_recv.at[pl.ds(0, REP - 1)], step_sems.at[1])
+    step_qkv = jnp.sum(step_recv[...], axis=0).astype(BF16)
+    loads[9].wait()
+    token = rows_of((8, HEAD_DIM))
+
+    def resident_weights(h):
+        row = rows_of((8, 512))
+        limit = jnp.zeros((8, 512), jnp.int32)
+        for b in range(4):
+            limit = jnp.where(row == b, lengths[b], limit)
+        scores = jnp.zeros((8, 512), F32)
+        for b in range(4):
+            keys = cache[b, 0, :, h * HEAD_DIM : (h + 1) * HEAD_DIM]
+            scores = jnp.where(row == b, score(take(0, h), keys), scores)
+        return weigh(scores, own_score(h), lanes_of((8, 512)) < limit)
+
+    def resident_mix(h, weights, weight_own):
+        mixed = jnp.zeros((8, HEAD_DIM), F32)
+        for b in range(4):
+            values = cache[b, 1, :, h * HEAD_DIM : (h + 1) * HEAD_DIM]
+            found = jnp.dot(weights, values, preferred_element_type=F32)
+            mixed = jnp.where(token == b, found, mixed)
+        mixed = mixed + weight_own * take(2, h).astype(F32)
+        mixed_res[rep, :, h * HEAD_DIM : (h + 1) * HEAD_DIM] = mixed.astype(BF16).astype(F32)
+
+    arrive(1, (-1, 2), (1, 2), (2, 2))
+    first = resident_weights(0)
     ring_step(0, 1)
     project(1)
     ring_step(1, 0)
     ring_step(0, 2)
-
-    wait_bytes(step_recv.at[pl.ds(0, REP - 1)], step_sems.at[1])
-    step_qkv = jnp.sum(step_recv[...], axis=0).astype(BF16)
-    loads[9].wait()
-    row = rows_of((8, 512))
-    limit = jnp.zeros((8, 512), jnp.int32)
-    for b in range(4):
-        limit = jnp.where(row == b, lengths[b], limit)
-    valid = lanes_of((8, 512)) < limit
-    token = rows_of((8, HEAD_DIM))
-    halves = []
-    for h in range(2):
-        span = slice(h * HEAD_DIM, (h + 1) * HEAD_DIM)
-        scores = jnp.zeros((8, 512), F32)
-        for b in range(4):
-            scores = jnp.where(row == b, score(take(0, h), cache[b, 0, :, span]), scores)
-        weights, weight_own = weigh(scores, own_score(h), valid)
-        mixed = jnp.zeros((8, HEAD_DIM), F32)
-        for b in range(4):
-            found = jnp.dot(weights, cache[b, 1, :, span], preferred_element_type=F32)
-            mixed = jnp.where(token == b, found, mixed)
-        halves.append(mixed + weight_own * take(2, h).astype(F32))
-    mixed_res[rep] = jnp.concatenate(halves, axis=1).astype(BF16).astype(F32)
+    resident_mix(0, *first)
+    second = resident_weights(1)
+    ring_step(1, 1)
+    resident_mix(1, *second)
     to_rep(lambda peer: push(mixed_res.at[rep], mixed_res.at[rep], mres_sems, (peer, head)))
-
-    ring_step(1, 1)
     ring_step(0, 3)
+    ring_step(1, 2)
+    totals0 = ring_end(0)
 
     wait_bytes(mixed_res.at[pl.ds(0, REP - 1)], mres_sems.at[1])
     loads[10].wait()
@@ -490,13 +510,9 @@
     update = jnp.dot(every, w_out[...], preferred_element_type=F32)
     mine = swap_halves(update, res_swap, res_sems)
 
-    ring_step(1, 2)
-    totals0 = ring_end(0)
+    ring_step(1, 3)
     sum_over_z(mine, res_swap, res_z, res_sems)
-    ring_step(1, 3)
-    sum_over_x(res_z, res_x, res_sems)
     totals1 = ring_end(1)
-    join(res_x, res_fin, res_sems)
 
     live = paused_count[partner[rep]]
     keyval = []
@@ -525,11 +541,8 @@
     mixed_mig[rep] = jnp.concatenate(halves, axis=0).astype(BF16).astype(F32)
     to_rep(lambda peer: push(mixed_mig.at[rep], mixed_mig.at[rep], mmig_sems, (peer, head)))
 
-    resident = joined(res_fin, res_sems)
-    row, col = rows_of((ROWS, 64)), lanes_of((ROWS, 64))
-    spread_rows = jnp.where((row // NQ) * 4 + lax.rem(row, NQ) == col, 1.0, 0.0)
-    spread_rows = jnp.where(lax.rem(row, NQ) < 4, spread_rows, 0.0).astype(BF16)
-    resident = jnp.dot(spread_rows, resident, preferred_element_type=F32)
+    sum_over_x(res_z, res_x, res_sems)
+    join(res_x, res_fin, res_sems)
 
     wait_bytes(mixed_mig.at[pl.ds(0, REP - 1)], mmig_sems.at[1])
     every = mixed_mig[...].reshape(128, HEAD_DIM).astype(BF16)
@@ -543,6 +556,13 @@
         )
     mine = swap_halves(update, mig_swap, mig_sems)
     sum_over_z(mine, mig_swap, mig_z, mig_sems)
+
+    resident = joined(res_fin, res_sems)
+    row, col = rows_of((ROWS, 64)), lanes_of((ROWS, 64))
+    spread_rows = jnp.where((row // NQ) * 4 + lax.rem(row, NQ) == col, 1.0, 0.0)
+    spread_rows = jnp.where(lax.rem(row, NQ) < 4, spread_rows, 0.0).astype(BF16)
+    resident = jnp.dot(spread_rows, resident, preferred_element_type=F32)
+
     sum_over_x(mig_z, mig_x, mig_sems)
     join(mig_x, mig_fin, mig_sems)
     migrated = joined(mig_fin, mig_sems)
@@ -558,8 +578,8 @@
     wait_bytes(mixed_res.at[pl.ds(0, REP - 1)], mres_sems.at[0])
     wait_bytes(mixed_mig.at[pl.ds(0, REP - 1)], mmig_sems.at[0])
     for p in range(2):
-        wait_bytes(gathered.at[p, pl.ds(0, 15)], ag_send.at[p])
-        wait_bytes(gathered.at[p, pl.ds(0, 16)], row_send.at[p])
+        wait_bytes(gathered[p].at[pl.ds(0, 15)], ag_send.at[p])
+        wait_bytes(gathered[p].at[pl.ds(0, 16)], row_send.at[p])
         for k in range(2):
             wait_bytes(pair_send[p].at[k], pair_ssem.at[p, k])
             for way in range(2):
@@ -620,7 +640,8 @@
             pltpu.VMEM((4, 2, 512, 256), BF16),
             pltpu.VMEM((REP, 8, 128), F32),
             pltpu.VMEM((HEAD, 8, 128), F32),
-            pltpu.VMEM((2, HEAD, PIECE, FEATS), BF16),
+            pltpu.VMEM((HEAD, KEEP[0], FEATS), BF16),
+            pltpu.VMEM((HEAD, 2 * KEEP[1], FEATS // 2), BF16),
             pltpu.VMEM((2, REP, KEEP[0], 512), F32),
             pltpu.VMEM((2, REP, KEEP[1], 512), F32),
             pltpu.VMEM((REP, 8, FEATS), F32),

time: 92.8 us -> 89.1 us (0.960)
  Pallas kernels: 88.8 us -> 85 us
    pallas_call x1, Pallas kernels: 88.8 us -> 85 us  [on_device(): pl.pallas_call(kernel, out_shape=(jax.ShapeDtypeStruct((2, MIG, 256), BF1...]
where the time goes in v3:
time: 89.1 us; the launch traced here: 88.9 us
  Pallas kernels  85 us (95%)
  local copies, waits for them, and re-layouts  3.19 us (4%)
    pallas_call x1, Pallas kernels, on_device(): pl.pallas_call(kernel, out_shape=(jax.ShapeDtypeStruct((2, MIG, 256), BF1...  85 us
    unnamed x2, local copies, waits for them, and re-layouts  3.19 us

profile of v3, /device:TPU:1, one launch (start us, length us, event | category | flops | bytes accessed | tf_op | source)
XLA Modules:
  0.0 88.9 jit_solution(3840606482585494451)
XLA Ops:
  0.6 85.0 %sublayer.1 = (bf16[2,112,256]{2,1,0:T(8,128)(2,1)}, bf16[80,768]{1,0:T(8,128)(2,1)}) custom-call(s32[16]{0:T(128)} %partner_hbm.1, s32[16]{0:T(128)} %count_hbm.1, s32[4]{0:T(128)} %lengths_hbm.1, bf16[80,768]{1,0:T(8,128)(2,1)} %step_hbm.1, bf16[56,768]{1,0:T(8,128)(2,1)} %paused_hbm.1, f32[768]{0:T(1024)} %gain_hbm.1, f32[768]{0:T(1024)} %bias_hbm.1, ...), custom_call_target="tpu_custom_call" | custom-call | tf_op jit(solution)/shard_map/sublayer/pallas_call | solution.py:620
  85.7 1.6 %copy.13 = bf16[112,2,256]{2,1,0:T(2,128)(2,1)} copy(bf16[112,2,256]{2,0,1:T(8,128)(2,1)} %bitcast.1) | data formatting | bytes 229376
  87.3 1.6 %copy.15 = bf16[80,768]{1,0:T(8,128)(2,1)} copy(bf16[80,768]{1,0:T(8,128)(2,1)} %get-tuple-element.11) | data formatting | bytes 245760
